TPU v7x, 32 devices: a whole 2x2x4 slice. The times are simulated.
32 devices in a mesh: grp: 4 (over y, core), blk: 8 (over z, x).
Axes of the slice: x: 2, y: 2, z: 4, core: 2. Of those that a mesh axis runs over, the one named last changes fastest.
Arguments:
- hidden_in: bfloat16 [8, 512, 1024], P('blk', 'grp'), may hold values from -6 to 6
- attn_gain: float32 [1024], replicated, may hold values from 0.1 to 1.9
- qkv_weight: bfloat16 [1024, 3, 16, 64], P(None, None, 'grp'), may hold values from -0.09375 to 0.09375
- rel_bias: float32 [32, 16], P(None, 'grp'), may hold values from -4 to 4
- prefix_cache: bfloat16 [8, 256, 2, 16, 64], P('blk', None, None, 'grp'), may hold values from -34 to 34
- prefix_owner: int32 [8], replicated, may hold values from 0 to 7, each once
- req_prefix: int32 [8, 2], replicated, may hold values from 0 to 7
- req_pages: int32 [8, 2], replicated, may hold values from 1 to 12, 16 in all within a row
- page_table: int32 [8, 16], replicated, may hold values from 0 to 15, each once within a row
- proj_weight: bfloat16 [1024, 1024], replicated, may hold values from -0.1875 to 0.1875
- mlp_gain: float32 [1024], replicated, may hold values from 0.1 to 1.9
- in_weight: bfloat16 [1024, 4096], P(None, 'grp'), may hold values from -0.1875 to 0.1875
- out_weight: bfloat16 [4096, 1024], P('grp'), may hold values from -0.09375 to 0.09375
Outputs:
- hidden_out: bfloat16 [8, 512, 1024], P('blk', 'grp')
- suffix_cache: bfloat16 [8, 512, 2, 16, 64], P('blk', None, None, 'grp')
Inputs may be any that keep to these rules, and one draw needn't show every extreme that they name: Prefix p's keys and values are row prefix_owner[p] of prefix_cache; every owner column holds one prefix. `req_pages`: each row sums to 16 and no entry exceeds 12. `page_table`: each row is a permutation of the logical pages of a column.
All inputs are finite; a program needn't handle non-finite values.
Results may differ from a plain program's by a relative error of at most 0.012.
Values may be sent and summed in bfloat16 or wider, within the bound.
A program may use at most 128 MiB of HBM per device.

v0:
```python
import jax
import jax.numpy as jnp
from jax import lax
from jax.sharding import PartitionSpec as P

PAGE = 32
EPSILON = 1e-06
THRESHOLDS = (12, 16, 23, 32, 46, 64, 91)


def rms_scale(values, gain):
    mean_sq = jnp.mean(values * values, axis=-1, keepdims=True)
    return values * lax.rsqrt(mean_sq + EPSILON) * gain


def bucket_of(relative):
    magnitude = jnp.abs(relative)
    steps_up = jnp.zeros(relative.shape, jnp.int32)
    for limit in THRESHOLDS:
        steps_up = steps_up + (magnitude >= limit).astype(jnp.int32)
    bucket = jnp.where(magnitude < 8, magnitude, jnp.minimum(8 + steps_up, 15))
    return bucket + 16 * (relative > 0).astype(jnp.int32)


def token_meta(pages_row, lengths_row, page_size, prefix_len):
    inclusive = jnp.cumsum(lengths_row, dtype=jnp.int32)
    exclusive = inclusive - lengths_row
    request = jnp.sum(
        (pages_row[:, None] >= inclusive[None, :]).astype(jnp.int32), axis=1, dtype=jnp.int32
    )
    slot_ids = jnp.arange(lengths_row.shape[0], dtype=jnp.int32)
    start = jnp.sum(
        jnp.where(request[:, None] == slot_ids[None, :], exclusive[None, :], 0),
        axis=1,
        dtype=jnp.int32,
    )
    offsets = (pages_row - start) * page_size + prefix_len
    within = jnp.arange(page_size, dtype=jnp.int32)
    positions = (offsets[:, None] + within[None, :]).reshape(-1)
    requests = jnp.broadcast_to(request[:, None], (request.shape[0], page_size)).reshape(-1)
    return (requests, positions)


def attend_block(queries, key_rows, value_rows, query_req, query_pos, key_req, key_pos, rel_bias):
    scores = jnp.einsum("qhd,khd->hqk", queries, key_rows, preferred_element_type=jnp.float32)
    bucket = bucket_of(key_pos[None, :] - query_pos[:, None])
    bias_add = jnp.zeros(scores.shape, jnp.float32)
    for bucket_id in range(rel_bias.shape[0]):
        bias_add = jnp.where(
            (bucket == bucket_id)[None], rel_bias[bucket_id][:, None, None], bias_add
        )
    allowed = (key_req[None, :] == query_req[:, None])[None]
    scores = jnp.where(allowed, scores + bias_add, -1e30)
    row_max = jnp.max(scores, axis=-1, keepdims=True)
    weights = jnp.exp(scores - row_max)
    weights = (weights / jnp.sum(weights, axis=-1, keepdims=True)).astype(jnp.bfloat16)
    return jnp.einsum(
        "hqk,khd->qhd", weights, value_rows, preferred_element_type=jnp.float32
    ).astype(jnp.bfloat16)


def shards(
    hidden_in,
    attn_gain,
    qkv_weight,
    rel_bias,
    prefix_cache,
    prefix_owner,
    req_prefix,
    req_pages,
    page_table,
    proj_weight,
    mlp_gain,
    in_weight,
    out_weight,
):
    width = hidden_in.shape[2]
    heads_dev = qkv_weight.shape[2]
    head_dim = qkv_weight.shape[3]
    inner = heads_dev * head_dim
    residual = hidden_in[0].astype(jnp.float32)
    normed = rms_scale(residual, attn_gain).astype(jnp.bfloat16)
    qkv_flat = qkv_weight.reshape(width, 3 * inner)
    projected = jnp.dot(
        lax.all_gather(normed, "grp", axis=0, tiled=True),
        qkv_flat,
        preferred_element_type=jnp.float32,
    ).astype(jnp.bfloat16)
    column_tok = projected.shape[0]
    projected = projected.reshape(column_tok, 3, heads_dev, head_dim)
    suffix_cache = projected[:, 1:3][None]
    column = lax.axis_index("blk")
    requests_col = req_prefix.shape[1]
    prefix_ids = jnp.arange(prefix_owner.shape[0], dtype=jnp.int32)
    owner_cols = jnp.sum(
        jnp.where(
            req_prefix[:, :, None] == prefix_ids[None, None, :], prefix_owner[None, None, :], 0
        ),
        axis=2,
        dtype=jnp.int32,
    )
    my_cols = lax.dynamic_index_in_dim(owner_cols, column, 0, keepdims=False)
    prefix_len = prefix_cache.shape[1]
    slot_width = 2 * inner
    local_slot = prefix_cache.reshape(prefix_len, slot_width)
    gathered = lax.all_gather(local_slot[None], "blk", axis=0, tiled=True)
    prefix_rows = jnp.take(gathered, my_cols, axis=0)
    prefix_rows = prefix_rows.reshape(requests_col * prefix_len, 2, heads_dev, head_dim)
    key_rows = jnp.concatenate([prefix_rows[:, 0], projected[:, 1]], axis=0)
    value_rows = jnp.concatenate([prefix_rows[:, 1], projected[:, 2]], axis=0)
    pages_row = lax.dynamic_index_in_dim(page_table, column, 0, keepdims=False)
    lengths_row = lax.dynamic_index_in_dim(req_pages, column, 0, keepdims=False)
    query_req, query_pos = token_meta(pages_row, lengths_row, PAGE, prefix_len)
    slot_ids = jnp.arange(requests_col, dtype=jnp.int32)
    key_req = jnp.concatenate([jnp.repeat(slot_ids, prefix_len), query_req])
    key_pos = jnp.concatenate(
        [jnp.tile(jnp.arange(prefix_len, dtype=jnp.int32), requests_col), query_pos]
    )
    block_rows = min(512, column_tok)
    block_count = column_tok // block_rows

    def one_block(operands):
        block_q, block_req, block_pos = operands
        return attend_block(
            block_q, key_rows, value_rows, block_req, block_pos, key_req, key_pos, rel_bias
        )

    attended = lax.map(
        one_block,
        (
            projected[:, 0].reshape(block_count, block_rows, heads_dev, head_dim),
            query_req.reshape(block_count, block_rows),
            query_pos.reshape(block_count, block_rows),
        ),
    )
    attended = attended.reshape(1, column_tok, inner)
    token_heads = lax.all_to_all(attended, "grp", split_axis=1, concat_axis=2, tiled=True)[0]
    mixed = residual + jnp.dot(token_heads, proj_weight, preferred_element_type=jnp.float32)
    normed_mlp = rms_scale(mixed, mlp_gain).astype(jnp.bfloat16)
    activated = jax.nn.relu(
        jnp.dot(
            lax.all_gather(normed_mlp, "grp", axis=0, tiled=True),
            in_weight,
            preferred_element_type=jnp.float32,
        )
    ).astype(jnp.bfloat16)
    summed = lax.psum_scatter(
        jnp.dot(activated, out_weight, preferred_element_type=jnp.float32).astype(jnp.bfloat16),
        "grp",
        scatter_dimension=0,
        tiled=True,
    ).astype(jnp.float32)
    hidden_out = (mixed + summed).astype(jnp.bfloat16)[None]
    return (hidden_out, suffix_cache)


def solution(mesh):
    return jax.shard_map(
        shards,
        mesh=mesh,
        in_specs=(
            P("blk", "grp", None),
            P(),
            P(None, None, "grp", None),
            P(None, "grp"),
            P("blk", None, None, "grp", None),
            P(),
            P(),
            P(),
            P(),
            P(),
            P(),
            P(None, "grp"),
            P("grp", None),
        ),
        out_specs=(P("blk", "grp", None), P("blk", None, None, "grp", None)),
        check_vma=False,
    )
```

profile of v0, /device:TPU:0, one launch (start us, length us, event | category | flops | bytes accessed | tf_op | source)
XLA Modules:
  0.0 208.7 jit_solution(3867273368891614869)
XLA Ops:
  7.2 1.2 fusion.11
  8.5 1.8 fusion.13
  10.3 1.8 copy.46
  12.2 0.9 select_reduce_fusion
  13.1 0.9 dynamic-slice_reduce_fusion
  14.0 1.9 slice_reduce_fusion.31
  15.9 1.6 slice_reduce_fusion.30
  19.7 1.2 broadcast_compare_fusion.32
  20.9 17.4 %broadcast_compare_fusion.25 = (pred[512,1024]{1,0:T(8,128)(4,1)}, pred[512,1024]{1,0:T(8,128)(4,1)}, pred[512,1024]{1,0:T(8,128)(4,1)}, pred[512,1024]{1,0:T(8,...) fusion(s32[512]{0:T(512)S(1)} %add.896, ...), kind=kLoop, calls=%fused_computation.47 | loop fusion | flops 31981568 | bytes 16783360 | tf_op jit(solution)/shard_map/while/body/eval_jaxpr/eq | solution.py:50
  38.3 3.7 %convolution_convert_fusion.1 = bf16[512,768]{1,0:T(8,128)(2,1)} fusion(bf16[512,1024]{1,0:T(8,128)(2,1)} %all-gather.6.cloned.1.call-done, bf16[1024,768]{0,1:T(8,128)(2,1)} %bitcast.76), kind=kOutput, calls=%fused_computation.19 | convolution fusion | flops 805699584 | bytes 3407872 | tf_op jit(solution)/shard_map/dot_general | solution.py:84
  42.1 1.4 copy.48
  43.5 0.8 slice_bitcast_fusion.5
  44.3 37.0 %all-gather.4.cloned.1.call-done = bf16[8,256,512]{2,1,0:T(8,128)(2,1)} async-done(((bf16[1,256,512]{2,1,0:T(8,128)(2,1)}), bf16[8,256,512]{2,1,0:T(8,128)(2,1)}) %all-gather.4.cloned.1.call-update) | async-done | bytes 2097168 | tf_op jit(solution)/shard_map/all_gather | solution.py:106
  81.3 2.2 %gather_fusion = bf16[2,256,512]{2,1,0:T(8,128)(2,1)S(1)} fusion(bf16[8,256,512]{2,1,0:T(8,128)(2,1)} %all-gather.4.cloned.1.call-done, s32[1024]{0:T(1024)S(1)} %pad_clamp_fusion), kind=kCustom, calls=%fused_computation | custom fusion | bytes 1048584 | tf_op jit(solution)/shard_map/jit(_take)/gather | solution.py:107
  83.5 1.1 copy.47
  84.6 1.4 gather.7
  86.1 29.9 %add_select_fusion = f32[4,512,1024]{2,1,0:T(8,128)} fusion(f32[4]{0:T(128)S(1)} %get-tuple-element.62, f32[4]{0:T(128)S(1)} %get-tuple-element.63, f32[4]{0:T(128)S(1)} %get-tuple-element.23, f32[4]{0:T(128)S(1)} %get-tuple-element.24, f32[4]{0:T(128)S(1)} %get-tuple-element.25, f32[4]{0:T(128)S(1)} %get-tuple-element.26, f32[4]{0:T(128)S(1)} %get-tuple-element.27, ...), kind=kOutput, calls=%fused_computation.4 | convolution fusion | flops 340787200 | bytes 26492928 | tf_op jit(solution)/shard_map/while/body/eval_jaxpr/qhd,khd->hqk/dot_general | solution.py:45
  116.0 7.5 %fusion.30 = f32[4,512]{1,0:T(4,128)S(1)} fusion(f32[4,512,1024]{2,1,0:T(8,128)} %add_select_fusion), kind=kOutput, calls=%fused_computation.138 | output fusion | flops 4195327 | bytes 8396800 | tf_op jit(solution)/shard_map/while/body/eval_jaxpr/sub | solution.py:55
  123.5 10.5 %fusion.10 = bf16[4,64,512]{2,1,0:T(8,128)(2,1)} fusion(f32[4,512]{1,0:T(4,128)S(1)} %fusion.30, bf16[512,4,64]{0,2,1:T(8,128)(2,1)S(1)} %copy-done.1, bf16[512,4,64]{0,2,1:T(8,128)(2,1)S(1)} %get-tuple-element.66, f32[4,512,1024]{2,1,0:T(8,128)} %add_select_fusion), kind=kOutput, calls=%fused_computation.21 | convolution fusion | flops 275909632 | bytes 9183232 | tf_op jit(solution)/shard_map/while/body/eval_jaxpr/hqk,khd->qhd/dot_general | solution.py:57
  134.0 1.3 copy.50
  135.8 2.9 %reduce.67 = bf16[512,256]{1,0:T(8,128)(2,1)} reduce(bf16[512,1,256]{2,1,0:T(2,128)(2,1)S(1)} %bitcast.69, bf16[]{:T(256)} %broadcast.2960), dimensions={1}, to_apply=%bitcast.52.reduce_sub_computation | reduce | bytes 524290
  138.8 1.0 reshape.1101
  139.8 9.1 %all_to_all.15 = bf16[4,2,16384]{2,1,0:T(2,128)(2,1)} all-to-all(bf16[4,2,16384]{2,1,0:T(2,128)(2,1)S(1)} %reshape.1101), channel_id=1, replica_groups=mesh['grp'=4,'blk'=8] {'grp'}, dimensions={0} | all-to-all | bytes 524288 | tf_op jit(solution)/shard_map/all_to_all | solution.py:137
  148.9 1.2 reshape.1102
  150.8 1.8 copy.51
  152.6 2.2 %multiply_reduce_fusion = (f32[128]{0:T(128)S(1)}, f32[128,1024]{1,0:T(8,128)S(1)}) fusion(bf16[128,1024]{0,1:T(8,128)(2,1)} %bitcast.71, bf16[1024,1024]{1,0:T(8,128)(2,1)} %param.22, bf16[1,128,1024]{2,1,0:T(8,128)(2,1)} %param.13), kind=kOutput, calls=%fused_computation.69 | convolution fusion | flops 268959616 | bytes 3146240 | tf_op jit(solution)/shard_map/dot_general | solution.py:138
  154.8 0.8 multiply_convert_fusion
  155.7 14.4 %all-gather.8.cloned.1.call-done = bf16[512,1024]{1,0:T(8,128)(2,1)} async-done(((bf16[128,1024]{1,0:T(8,128)(2,1)}), bf16[512,1024]{1,0:T(8,128)(2,1)}) %all-gather.8.cloned.1.call-update) | async-done | bytes 1048592 | tf_op jit(solution)/shard_map/all_gather | solution.py:142
  170.1 5.2 %convolution_convert_fusion = bf16[512,1024]{1,0:T(8,128)(2,1)} fusion(bf16[1024,1024]{1,0:T(8,128)(2,1)S(1)} %copy-done, bf16[512,1024]{1,0:T(8,128)(2,1)} %all-gather.8.cloned.1.call-done, bf16[1024,1024]{1,0:T(8,128)(2,1)} %param.24), kind=kOutput, calls=%fused_computation.18 | convolution fusion | flops 2149056512 | bytes 6291456 | tf_op jit(solution)/shard_map/dot_general | solution.py:148
  175.4 0.8 slice_bitcast_fusion
  176.2 24.2 %reduce-scatter.2.cloned.1.call-done = bf16[128,1024]{1,0:T(8,128)(2,1)} async-done(((bf16[512,1024]{1,0:T(8,128)(2,1)}), bf16[128,1024]{1,0:T(8,128)(2,1)}) %reduce-scatter.2.cloned.1.call-update) | async-done | bytes 262160 | tf_op jit(solution)/shard_map/reduce_scatter | solution.py:147
  200.4 1.7 fusion.20
  (43 shorter events, 3.9 us)
Async XLA Ops:
  7.2 163.0 %copy-start = (bf16[1024,1024]{1,0:T(8,128)(2,1)S(1)}, bf16[1024,1024]{1,0:T(8,128)(2,1)}, u32[]{:S(2)}) copy-start(bf16[1024,1024]{1,0:T(8,128)(2,1)} %param.25) | copy-start | bytes 6291460
  7.2 31.1 %all-gather.6.cloned.1.call-start = ((), (), s32[]{:S(2)}) async-start(), calls=%async_computation.3 | async-start | bytes 1310720 | tf_op jit(solution)/shard_map/all_gather | solution.py:85
  10.3 71.0 %all-gather.4.cloned.1.call-start = ((), (), s32[]{:S(2)}) async-start(), calls=%async_computation.2 | async-start | bytes 2359296 | tf_op jit(solution)/shard_map/all_gather | solution.py:106
  12.2 158.0 %all-gather.8.cloned.1.call-start = ((), (), s32[]{:S(2)}) async-start(), calls=%async_computation.4 | async-start | bytes 1310720 | tf_op jit(solution)/shard_map/all_gather | solution.py:142
  116.0 7.5 %copy-start.1 = (bf16[512,4,64]{0,2,1:T(8,128)(2,1)S(1)}, bf16[512,4,64]{0,2,1:T(8,128)(2,1)}, u32[]{:S(2)}) copy-start(bf16[512,4,64]{0,2,1:T(8,128)(2,1)} %get-tuple-element.64) | copy-start | bytes 786436
  150.1 4.8 %copy-start.2 = (f32[1024]{0:T(1024)S(1)}, f32[1024]{0:T(1024)}, u32[]{:S(2)}) copy-start(f32[1024]{0:T(1024)} %param.23) | copy-start | bytes 12292
  155.7 44.8 %reduce-scatter.2.cloned.1.call-start = ((), (), s32[]{:S(2)}) async-start(), calls=%async_computation.5 | async-start | bytes 1310720 | tf_op jit(solution)/shard_map/reduce_scatter | solution.py:147
Sparse Core Ops, SparseCore 0:
  10.4 19.4 all-gather.5
  32.0 49.2 all-gather.3
  155.8 14.2 all-gather.7
  175.5 24.8 reduce-scatter.1
where the time goes:
time: 209 us
  waiting for transfers between devices  75.7 us (36%)
  matrix products  51.6 us (25%)
  other arithmetic  36.6 us (18%)
  local copies, waits for them, and re-layouts  21.6 us (10%)
  between operations  13.9 us (7%)
  blocking collectives  9.1 us (4%)
    all_gather x1, waiting for transfers between devices, shards(): gathered = lax.all_gather(local_slot[None], 'blk', axis=0, tiled=True)  37 us
    dot_general x1, matrix products, attend_block(): jnp.einsum('qhd,khd->hqk', queries, key_rows, preferred_element_type=jnp....  29.9 us
    reduce_scatter x1, waiting for transfers between devices, shards(): lax.psum_scatter(jnp.dot(activated, out_weight, preferred_element_type=jn...  24.2 us
    eq x1, other arithmetic, attend_block(): bucket == bucket_id  17.4 us
    all_gather x1, waiting for transfers between devices, shards(): lax.all_gather(normed_mlp, 'grp', axis=0, tiled=True)  14.4 us
    dot_general x1, matrix products, attend_block(): jnp.einsum('hqk,khd->qhd', weights, value_rows, preferred_element_type=jn...  10.5 us
    all_to_all x1, blocking collectives, shards(): lax.all_to_all(attended, 'grp', split_axis=1, concat_axis=2, tiled=True)[0]  9.1 us
    sub x1, other arithmetic, attend_block(): weights = jnp.exp(scores - row_max)  7.51 us
  transfers between devices with their start and end apart: 4, of which 3 were waited for; matrix products, arithmetic and copies ran while one was open for 17% of the time, Pallas kernels for 0%

commit v1 on v0

--- a/solution.py
+++ b/solution.py
@@ -134,7 +134,10 @@
         ),
     )
     attended = attended.reshape(1, column_tok, inner)
-    token_heads = lax.all_to_all(attended, "grp", split_axis=1, concat_axis=2, tiled=True)[0]
+    token_heads = jnp.concatenate(
+        lax.all_to_all(jnp.stack(jnp.split(attended, lax.axis_size("grp"), axis=1)), "grp", 0, 0),
+        axis=2,
+    )[0]
     mixed = residual + jnp.dot(token_heads, proj_weight, preferred_element_type=jnp.float32)
     normed_mlp = rms_scale(mixed, mlp_gain).astype(jnp.bfloat16)
     activated = jax.nn.relu(

time: 209 us -> 199 us (0.952)
  local copies, waits for them, and re-layouts: 21.6 us -> 15.8 us
  other arithmetic: 36.6 us -> 33.7 us
    unnamed x15 -> x11, local copies, waits for them, and re-layouts: 3.57 us -> 0.13 us
    unnamed x1 -> x0, other arithmetic: 2.91 us -> none
where the time goes in v1:
time: 199 us
  waiting for transfers between devices  75.7 us (38%)
  matrix products  50.8 us (26%)
  other arithmetic  33.7 us (17%)
  local copies, waits for them, and re-layouts  15.8 us (8%)
  between operations  13.9 us (7%)
  blocking collectives  8.58 us (4%)
    all_gather x1, waiting for transfers between devices, shards(): gathered = lax.all_gather(local_slot[None], 'blk', axis=0, tiled=True)  37 us
    dot_general x1, matrix products, attend_block(): jnp.einsum('qhd,khd->hqk', queries, key_rows, preferred_element_type=jnp....  29.8 us
    reduce_scatter x1, waiting for transfers between devices, shards(): lax.psum_scatter(jnp.dot(activated, out_weight, preferred_element_type=jn...  24.2 us
    eq x1, other arithmetic, attend_block(): bucket == bucket_id  17.4 us
    all_gather x1, waiting for transfers between devices, shards(): lax.all_gather(normed_mlp, 'grp', axis=0, tiled=True)  14.4 us
    dot_general x1, matrix products, attend_block(): jnp.einsum('hqk,khd->qhd', weights, value_rows, preferred_element_type=jn...  9.86 us
    all_to_all x1, blocking collectives, shards(): lax.all_to_all(jnp.stack(jnp.split(attended, lax.axis_size('grp'), axis=1...  8.58 us
    sub x1, other arithmetic, attend_block(): weights = jnp.exp(scores - row_max)  7.51 us
  transfers between devices with their start and end apart: 4, of which 3 were waited for; matrix products, arithmetic and copies ran while one was open for 17% of the time, Pallas kernels for 0%

profile of v1, /device:TPU:0, one launch (start us, length us, event | category | flops | bytes accessed | tf_op | source)
XLA Modules:
  0.0 198.7 jit_solution(17946273878418214235)
XLA Ops:
  7.2 1.2 fusion.11
  8.5 1.8 fusion.13
  10.3 1.8 copy.40
  12.2 0.9 select_reduce_fusion
  13.1 0.9 dynamic-slice_reduce_fusion
  14.0 1.9 slice_reduce_fusion.31
  15.9 1.6 slice_reduce_fusion.30
  17.5 0.1 copy.44
  17.6 0.2 reduce-window.4
  17.8 0.7 fusion.23
  18.6 0.7 multiply_add_fusion
  19.7 1.2 broadcast_compare_fusion.32
  20.9 17.4 %broadcast_compare_fusion.25 = (pred[512,1024]{1,0:T(8,128)(4,1)}, pred[512,1024]{1,0:T(8,128)(4,1)}, pred[512,1024]{1,0:T(8,128)(4,1)}, pred[512,1024]{1,0:T(8,...) fusion(s32[512]{0:T(512)S(1)} %add.896, ...), kind=kLoop, calls=%fused_computation.47 | loop fusion | flops 31981568 | bytes 16783360 | tf_op jit(solution)/shard_map/while/body/eval_jaxpr/eq | solution.py:50
  38.3 3.7 %convolution_convert_fusion.1 = bf16[512,768]{1,0:T(8,128)(2,1)} fusion(bf16[512,1024]{1,0:T(8,128)(2,1)} %all-gather.6.cloned.1.call-done, bf16[1024,768]{0,1:T(8,128)(2,1)} %bitcast.78), kind=kOutput, calls=%fused_computation.19 | convolution fusion | flops 805699584 | bytes 3407872 | tf_op jit(solution)/shard_map/dot_general | solution.py:84
  42.1 1.4 copy.42
  43.5 0.8 slice_bitcast_fusion.5
  44.3 37.0 %all-gather.4.cloned.1.call-done = bf16[8,256,512]{2,1,0:T(8,128)(2,1)} async-done(((bf16[1,256,512]{2,1,0:T(8,128)(2,1)}), bf16[8,256,512]{2,1,0:T(8,128)(2,1)}) %all-gather.4.cloned.1.call-update) | async-done | bytes 2097168 | tf_op jit(solution)/shard_map/all_gather | solution.py:106
  81.3 2.2 %gather_fusion = bf16[2,256,512]{2,1,0:T(8,128)(2,1)S(1)} fusion(bf16[8,256,512]{2,1,0:T(8,128)(2,1)} %all-gather.4.cloned.1.call-done, s32[1024]{0:T(1024)S(1)} %pad_clamp_fusion), kind=kCustom, calls=%fused_computation | custom fusion | bytes 1048584 | tf_op jit(solution)/shard_map/jit(_take)/gather | solution.py:107
  83.5 1.1 copy.41
  84.6 1.4 gather.7
  86.0 0.7 slice_bitcast_fusion.6
  86.8 29.8 %add_select_fusion = f32[4,512,1024]{2,1,0:T(8,128)} fusion(f32[4]{0:T(128)S(1)} %get-tuple-element.62, f32[4]{0:T(128)S(1)} %get-tuple-element.63, f32[4]{0:T(128)S(1)} %get-tuple-element.23, f32[4]{0:T(128)S(1)} %get-tuple-element.24, f32[4]{0:T(128)S(1)} %get-tuple-element.25, f32[4]{0:T(128)S(1)} %get-tuple-element.26, f32[4]{0:T(128)S(1)} %get-tuple-element.27, ...), kind=kOutput, calls=%fused_computation.4 | convolution fusion | flops 340787200 | bytes 26492928 | tf_op jit(solution)/shard_map/while/body/eval_jaxpr/qhd,khd->hqk/dot_general | solution.py:45
  116.6 7.5 %fusion.30 = f32[4,512]{1,0:T(4,128)S(1)} fusion(f32[4,512,1024]{2,1,0:T(8,128)} %add_select_fusion), kind=kOutput, calls=%fused_computation.143 | output fusion | flops 4195327 | bytes 8396800 | tf_op jit(solution)/shard_map/while/body/eval_jaxpr/sub | solution.py:55
  124.1 9.9 %fusion.10 = bf16[4,64,512]{2,1,0:T(8,128)(2,1)S(1)} fusion(f32[4,512]{1,0:T(4,128)S(1)} %fusion.30, bf16[512,4,64]{0,2,1:T(8,128)(2,1)S(1)} %copy-done.1, bf16[512,4,64]{0,2,1:T(8,128)(2,1)} %get-tuple-element.66, f32[4,512,1024]{2,1,0:T(8,128)} %add_select_fusion), kind=kOutput, calls=%fused_computation.21 | convolution fusion | flops 275909632 | bytes 9183232 | tf_op jit(solution)/shard_map/while/body/eval_jaxpr/hqk,khd->qhd/dot_general | solution.py:57
  134.1 8.6 %all_to_all.5 = bf16[4,1,128,256]{2,3,1,0:T(8,128)(2,1)S(1)} all-to-all(bf16[4,1,128,256]{2,3,1,0:T(8,128)(2,1)S(1)} %pad_maximum_fusion), channel_id=1, replica_groups=mesh['grp'=4,'blk'=8] {'grp'}, dimensions={0} | all-to-all | bytes 524288 | tf_op jit(solution)/shard_map/all_to_all | solution.py:138
  142.7 2.1 %multiply_reduce_fusion = (f32[128]{0:T(128)S(1)}, f32[128,1024]{1,0:T(8,128)S(1)}) fusion(bf16[128,1024]{0,1:T(8,128)(2,1)S(1)} %bitcast.73, bf16[1024,1024]{1,0:T(8,128)(2,1)} %param.22, bf16[1,128,1024]{2,1,0:T(8,128)(2,1)} %param.13), kind=kOutput, calls=%fused_computation.69 | convolution fusion | flops 268959616 | bytes 3146240 | tf_op jit(solution)/shard_map/dot_general | solution.py:141
  144.8 0.8 multiply_convert_fusion
  145.7 14.4 %all-gather.8.cloned.1.call-done = bf16[512,1024]{1,0:T(8,128)(2,1)} async-done(((bf16[128,1024]{1,0:T(8,128)(2,1)}), bf16[512,1024]{1,0:T(8,128)(2,1)}) %all-gather.8.cloned.1.call-update) | async-done | bytes 1048592 | tf_op jit(solution)/shard_map/all_gather | solution.py:145
  160.1 5.2 %convolution_convert_fusion = bf16[512,1024]{1,0:T(8,128)(2,1)} fusion(bf16[1024,1024]{1,0:T(8,128)(2,1)S(1)} %copy-done, bf16[512,1024]{1,0:T(8,128)(2,1)} %all-gather.8.cloned.1.call-done, bf16[1024,1024]{1,0:T(8,128)(2,1)} %param.24), kind=kOutput, calls=%fused_computation.18 | convolution fusion | flops 2149056512 | bytes 6291456 | tf_op jit(solution)/shard_map/dot_general | solution.py:151
  165.4 0.8 slice_bitcast_fusion
  166.3 24.2 %reduce-scatter.2.cloned.1.call-done = bf16[128,1024]{1,0:T(8,128)(2,1)} async-done(((bf16[512,1024]{1,0:T(8,128)(2,1)}), bf16[128,1024]{1,0:T(8,128)(2,1)}) %reduce-scatter.2.cloned.1.call-update) | async-done | bytes 262160 | tf_op jit(solution)/shard_map/reduce_scatter | solution.py:150
  190.5 1.7 fusion.20
  (38 shorter events, 1.0 us)
Async XLA Ops:
  7.2 153.0 %copy-start = (bf16[1024,1024]{1,0:T(8,128)(2,1)S(1)}, bf16[1024,1024]{1,0:T(8,128)(2,1)}, u32[]{:S(2)}) copy-start(bf16[1024,1024]{1,0:T(8,128)(2,1)} %param.25) | copy-start | bytes 6291460
  7.2 31.1 %all-gather.6.cloned.1.call-start = ((), (), s32[]{:S(2)}) async-start(), calls=%async_computation.3 | async-start | bytes 1310720 | tf_op jit(solution)/shard_map/all_gather | solution.py:85
  10.3 71.0 %all-gather.4.cloned.1.call-start = ((), (), s32[]{:S(2)}) async-start(), calls=%async_computation.2 | async-start | bytes 2359296 | tf_op jit(solution)/shard_map/all_gather | solution.py:106
  12.2 148.0 %all-gather.8.cloned.1.call-start = ((), (), s32[]{:S(2)}) async-start(), calls=%async_computation.4 | async-start | bytes 1310720 | tf_op jit(solution)/shard_map/all_gather | solution.py:145
  116.6 7.5 %copy-start.1 = (bf16[512,4,64]{0,2,1:T(8,128)(2,1)S(1)}, bf16[512,4,64]{0,2,1:T(8,128)(2,1)}, u32[]{:S(2)}) copy-start(bf16[512,4,64]{0,2,1:T(8,128)(2,1)} %get-tuple-element.64) | copy-start | bytes 786436
  134.0 10.8 %copy-start.2 = (f32[1024]{0:T(1024)S(1)}, f32[1024]{0:T(1024)}, u32[]{:S(2)}) copy-start(f32[1024]{0:T(1024)} %param.23) | copy-start | bytes 12292
  145.7 44.8 %reduce-scatter.2.cloned.1.call-start = ((), (), s32[]{:S(2)}) async-start(), calls=%async_computation.5 | async-start | bytes 1310720 | tf_op jit(solution)/shard_map/reduce_scatter | solution.py:150
Sparse Core Ops, SparseCore 0:
  10.4 19.4 all-gather.5
  32.0 49.2 all-gather.3
  145.8 14.2 all-gather.7
  165.5 24.8 reduce-scatter.1
